TPU v7x, 512 devices: a whole 4x8x8 slice. The times are simulated.
512 devices in a mesh: front: 8 (over x, y_hi), row: 8 (over z), col: 8 (over y_lo, core).
Axes of the slice: x: 4, y: 8 (y_hi: 2, y_lo: 4; y = y_hi * 4 + y_lo), z: 8, core: 2. Of those that a mesh axis runs over, the one named last changes fastest.
Arguments:
- parent_front: bfloat16 [8, 8192, 4096], P('front', 'row', 'col'), may hold values from -3 to 28, as said below
- child_front: bfloat16 [8, 4096, 4096], P('front', 'row', 'col'), may hold values from -2 to 2, as said below
- child_blocks: int32 [8, 16], replicated, may hold values from 0 to 31, as said below
- child_mask: int32 [8, 16, 16], replicated, may hold values from 0 to 1, as said below
Outputs:
- factored_front: float32 [8, 8192, 4096], P('front', 'row', 'col')
Inputs may be any that keep to these rules, and one draw needn't show every extreme that they name: `parent_front`: each parent's matrix is symmetric, and its sum with the extend-add of its two children's masked contributions is positive definite. `child_front`: each child's contribution is symmetric. `child_blocks`: for child c, the tiles a with a % 8 == r map to distinct parent tiles congruent to r modulo 8 that rise with a, and one of them is the last such parent tile. `child_mask`: symmetric in its last two dimensions, with ones on the diagonal.
All inputs are finite; a program needn't handle non-finite values.
Results may differ from a plain program's by a relative error of at most 0.0003.
Values may be sent and summed in bfloat16 or wider, within the bound.
No kernel may reach another device: no remote copies, remote signals or barrier semaphores. Data moves between devices by JAX's collectives and lax.ppermute only.
A program may use at most 64 MiB of HBM per device.

v0:
```python
import jax
import jax.numpy as jnp
from jax import lax
from jax.sharding import PartitionSpec as P

B = 256
PANELS = 2


def broadcast(block, axis, owner):
    block = jnp.where(lax.axis_index(axis) == owner, block, jnp.zeros_like(block))
    return lax.psum(block, axis)


def partner(block, axis, stride):
    count = lax.axis_size(axis)
    route = []
    for low in range(count):
        high = low | 1 << stride
        if high != low and high < count:
            route += [(low, high), (high, low)]
    return lax.ppermute(block, axis, route)


def extend_child(
    update,
    child_index,
    child_blocks,
    child_mask,
    grid_row,
    grid_col,
    half_index,
    row_slots,
    col_slots,
):
    row_count = lax.axis_size("row")
    col_count = lax.axis_size("col")
    crow_slots = update.shape[0] // B
    ccol_slots = update.shape[1] // B
    block_map = lax.dynamic_index_in_dim(child_blocks, child_index, 0, keepdims=False)
    tile_mask = lax.dynamic_index_in_dim(child_mask, child_index, 0, keepdims=False)
    map_down = lax.dynamic_index_in_dim(
        block_map.reshape(crow_slots, row_count), grid_row, 1, keepdims=False
    )
    map_across = lax.dynamic_index_in_dim(
        block_map.reshape(ccol_slots, col_count), grid_col, 1, keepdims=False
    )
    mask_band = lax.dynamic_index_in_dim(
        tile_mask.reshape(crow_slots, row_count, tile_mask.shape[1]), grid_row, 1, keepdims=False
    )
    mask_local = lax.dynamic_index_in_dim(
        mask_band.reshape(crow_slots, ccol_slots, col_count), grid_col, 2, keepdims=False
    )
    row_place = (map_down[None, :] // row_count == jnp.arange(row_slots)[:, None]).astype(
        jnp.bfloat16
    )
    col_match = (map_across[None, :] // (2 * col_count) == jnp.arange(col_slots)[:, None]) & (
        (map_across[None, :] // col_count + map_across[None, :]) % 2 == half_index
    )
    col_place = col_match.astype(jnp.bfloat16)
    tile_values = (
        update.reshape(crow_slots, B, ccol_slots, B)
        * mask_local.astype(jnp.bfloat16)[:, None, :, None]
    )
    placed = jnp.einsum(
        "xa,aibj,yb->xiyj", row_place, tile_values, col_place, preferred_element_type=jnp.float32
    )
    return placed.reshape(row_slots * B, col_slots * B)


def factor_column(column, step_index, grid_row, row_count, row_slots):
    first_row = step_index // row_count * B
    pivot_tile = broadcast(column[first_row : first_row + B], "row", step_index % row_count)
    pivot_factor = jnp.linalg.cholesky(pivot_tile)
    solved = lax.linalg.triangular_solve(
        pivot_factor, column, left_side=False, lower=True, transpose_a=True
    )
    block_global = jnp.arange(row_slots) * row_count + grid_row
    shaped = solved.reshape(row_slots, B, B)
    shaped = jnp.where(
        (block_global > step_index)[:, None, None],
        shaped,
        jnp.where((block_global == step_index)[:, None, None], pivot_factor[None], 0.0),
    )
    return shaped.reshape(row_slots * B, B)


def spread_rows(own_rows, step_index, half_index, col_count):
    owner_half = (step_index // col_count + step_index) % 2
    owner_col = step_index % col_count
    along_cols = broadcast(own_rows, "col", owner_col)
    across = partner(along_cols, "front", 0)
    return jnp.where(half_index == owner_half, along_cols, across)


def column_side(row_panel, half_index, grid_col, row_count, col_count, row_slots, col_slots):
    upper_half = (half_index + grid_col) % 2
    root_row = (upper_half * col_count + grid_col) % row_count
    wanted = (
        jnp.arange(col_slots) * (2 * col_count) + upper_half * col_count + grid_col
    ) // row_count
    selector = (wanted[:, None] == jnp.arange(row_slots)[None, :]).astype(jnp.float32)
    chosen = jnp.einsum(
        "ut,tij->uij", selector, row_panel.reshape(row_slots, B, B), precision=lax.Precision.HIGHEST
    )
    return broadcast(chosen.reshape(col_slots * B, B), "row", root_row)


def trailing(slab, row_panel, col_panel, step_index, row_global, col_global):
    product = lax.dot_general(
        row_panel,
        col_panel,
        (((1,), (1,)), ((), ())),
        precision=lax.Precision.HIGHEST,
        preferred_element_type=jnp.float32,
    )
    slot_count = col_global.shape[0]
    slab_blocks = slab.reshape(slab.shape[0], slot_count, B)
    product_blocks = product.reshape(slab.shape[0], slot_count, B)
    row_later = jnp.repeat(row_global > step_index, B)[:, None, None]
    col_later = (col_global > step_index)[None, :, None]
    col_now = (col_global == step_index)[None, :, None]
    merged = jnp.where(
        col_later,
        jnp.where(row_later, slab_blocks - product_blocks, 0.0),
        jnp.where(col_now, row_panel[:, None, :], slab_blocks),
    )
    return merged.reshape(slab.shape)


def on_device(parent_front, child_front, child_blocks, child_mask):
    row_count = lax.axis_size("row")
    col_count = lax.axis_size("col")
    group_index = lax.axis_index("front")
    grid_row = lax.axis_index("row")
    grid_col = lax.axis_index("col")
    half_index = group_index % 2
    sibling = group_index + 1 - 2 * half_index
    local_front = parent_front[0].astype(jnp.float32)
    row_slots = local_front.shape[0] // B
    col_slots = local_front.shape[1] // B
    own_child = child_front[0]
    other_child = partner(own_child, "front", 0)
    local_front = local_front + extend_child(
        own_child,
        group_index,
        child_blocks,
        child_mask,
        grid_row,
        grid_col,
        half_index,
        row_slots,
        col_slots,
    )
    local_front = local_front + extend_child(
        other_child,
        sibling,
        child_blocks,
        child_mask,
        grid_row,
        grid_col,
        half_index,
        row_slots,
        col_slots,
    )
    row_global = jnp.arange(row_slots) * row_count + grid_row
    col_global = (
        jnp.arange(col_slots) * (2 * col_count) + (half_index + grid_col) % 2 * col_count + grid_col
    )
    for step_index in range(PANELS):
        slot_index = step_index // (2 * col_count)
        own_rows = factor_column(
            local_front[:, slot_index * B : (slot_index + 1) * B],
            step_index,
            grid_row,
            row_count,
            row_slots,
        )
        row_panel = spread_rows(own_rows, step_index, half_index, col_count)
        col_panel = column_side(
            row_panel, half_index, grid_col, row_count, col_count, row_slots, col_slots
        )
        local_front = trailing(
            local_front, row_panel, col_panel, step_index, row_global, col_global
        )
    return local_front[None]


def solution(mesh):
    return jax.shard_map(
        on_device,
        mesh=mesh,
        in_specs=(P("front", "row", "col"), P("front", "row", "col"), P(), P()),
        out_specs=P("front", "row", "col"),
        check_vma=False,
    )
```

profile of v0, /device:TPU:2, one launch (start us, length us, event | category | flops | bytes accessed | tf_op | source)
XLA Modules:
  0.0 817.8 jit_solution(14027624428790879510)
XLA Ops:
  6.5 7.7 collective-permute-start
  19.6 2.3 convolution_bitcast_fusion.1
  22.6 3.2 copy.21
  25.9 1.8 copy.45
  28.0 9.0 %collective-permute-done = bf16[512,512]{1,0:T(8,128)(2,1)} collective-permute-done((bf16[512,512]{1,0:T(8,128)(2,1)}, bf16[512,512]{1,0:T(8,128)(2,1)}, u32[]{:S(2)}, u32[]{:S(2)}) %collective-permute-start) | collective-permute-done | bytes 524320 | tf_op jit(solution)/shard_map/ppermute | solution.py:22
  37.0 2.0 reshape.576
  39.0 1.8 fusion.17
  40.8 2.3 convolution_bitcast_fusion
  43.1 4.1 copy.22
  47.3 2.2 copy.46
  52.7 83.7 %all-reduce.8.cloned.1.call-done = f32[256,256]{0,1:T(8,128)} async-done(((f32[256,256]{0,1:T(8,128)}), f32[256,256]{0,1:T(8,128)}) %all-reduce.8.cloned.1.call-update) | async-done | bytes 262160 | tf_op jit(solution)/shard_map/psum | solution.py:12
  138.5 11.7 %cholesky.130 = f32[128,128]{1,0:T(8,128)S(1)} custom-call(f32[128,128]{1,0:T(8,128)S(1)} %cholesky.194), custom_call_target="Cholesky" | custom-call | tf_op jit(solution)/shard_map/jit(cholesky)/cholesky | solution.py:74
  150.9 9.8 %custom-call.13 = f32[1,128,128]{1,2,0:T(8,128)S(1)} custom-call(f32[1,128,128]{2,1,0:T(8,128)S(1)} %get-tuple-element.62), custom_call_target="InvertDiagBlocksLowerTriangular" | custom-call | tf_op jit(solution)/shard_map/jit(cholesky)/cholesky | solution.py:74
  161.2 11.7 %cholesky.147 = f32[128,128]{1,0:T(8,128)S(1)} custom-call(f32[128,128]{1,0:T(8,128)S(1)} %convolution_subtract_fusion.2), custom_call_target="Cholesky" | custom-call | tf_op jit(solution)/shard_map/jit(cholesky)/cholesky | solution.py:74
  175.2 4.2 while.4
  179.9 19.7 %custom-call.14 = f32[2,128,128]{1,2,0:T(8,128)S(1)} custom-call(f32[2,128,128]{2,1,0:T(8,128)S(1)} %get-tuple-element.21), custom_call_target="InvertDiagBlocksLowerTriangular" | custom-call | tf_op jit(solution)/shard_map/triangular_solve/custom-call.0 | solution.py:75
  199.6 1.7 fusion.15
  201.3 1.7 convolution_subtract_fusion
  205.2 77.4 %all-reduce.10.cloned.1.call-done = f32[1024,256]{0,1:T(8,128)} async-done(((f32[1024,256]{0,1:T(8,128)}), f32[1024,256]{0,1:T(8,128)}) %all-reduce.10.cloned.1.call-update) | async-done | bytes 1048592 | tf_op jit(solution)/shard_map/psum | solution.py:12
  282.6 5.5 collective-permute-start.1
  288.2 45.9 %collective-permute-done.1 = f32[1024,256]{0,1:T(8,128)} collective-permute-done((f32[1024,256]{0,1:T(8,128)}, f32[1024,256]{0,1:T(8,128)}, u32[]{:S(2)}, u32[]{:S(2)}) %collective-permute-start.1) | collective-permute-done | bytes 1048608 | tf_op jit(solution)/shard_map/ppermute | solution.py:22
  334.1 1.4 broadcast_select_fusion.1
  335.5 1.5 reshape.582
  336.9 2.3 copy.27
  339.2 2.3 convolution_select_fusion.1
  342.7 79.3 %all-reduce.12.cloned.1.call-done = f32[512,256]{1,0:T(8,128)} async-done(((f32[512,256]{1,0:T(8,128)}), f32[512,256]{1,0:T(8,128)}) %all-reduce.12.cloned.1.call-update) | async-done | bytes 524304 | tf_op jit(solution)/shard_map/psum | solution.py:12
  422.0 5.3 fusion.5
  430.0 76.2 %all-reduce.14.cloned.1.call-done = f32[256,256]{0,1:T(8,128)} async-done(((f32[256,256]{0,1:T(8,128)}), f32[256,256]{0,1:T(8,128)}) %all-reduce.14.cloned.1.call-update) | async-done | bytes 262160 | tf_op jit(solution)/shard_map/psum | solution.py:12
  508.9 11.7 %cholesky.164 = f32[128,128]{1,0:T(8,128)S(1)} custom-call(f32[128,128]{1,0:T(8,128)S(1)} %cholesky.197), custom_call_target="Cholesky" | custom-call | tf_op jit(solution)/shard_map/jit(cholesky)/cholesky | solution.py:74
  521.3 9.8 %custom-call.15 = f32[1,128,128]{1,2,0:T(8,128)S(1)} custom-call(f32[1,128,128]{2,1,0:T(8,128)S(1)} %get-tuple-element.58), custom_call_target="InvertDiagBlocksLowerTriangular" | custom-call | tf_op jit(solution)/shard_map/jit(cholesky)/cholesky | solution.py:74
  533.3 11.7 %cholesky.181 = f32[128,128]{1,0:T(8,128)S(1)} custom-call(f32[128,128]{1,0:T(8,128)S(1)} %convolution_subtract_fusion.1), custom_call_target="Cholesky" | custom-call | tf_op jit(solution)/shard_map/jit(cholesky)/cholesky | solution.py:74
  547.8 1.8 copy.32
  549.6 5.4 while.5
  555.7 20.5 %custom-call.16 = f32[2,128,128]{1,2,0:T(8,128)S(1)} custom-call(f32[2,128,128]{2,1,0:T(8,128)} %copy-done.10), custom_call_target="InvertDiagBlocksLowerTriangular" | custom-call | tf_op jit(solution)/shard_map/triangular_solve/custom-call.0 | solution.py:75
  576.2 1.7 fusion.13
  578.5 1.7 fusion.12
  581.9 77.3 %all-reduce.16.cloned.1.call-done = f32[1024,256]{0,1:T(8,128)} async-done(((f32[1024,256]{0,1:T(8,128)}), f32[1024,256]{0,1:T(8,128)}) %all-reduce.16.cloned.1.call-update) | async-done | bytes 1048592 | tf_op jit(solution)/shard_map/psum | solution.py:12
  659.2 5.5 collective-permute-start.2
  664.7 46.0 %collective-permute-done.2 = f32[1024,256]{0,1:T(8,128)} collective-permute-done((f32[1024,256]{0,1:T(8,128)}, f32[1024,256]{0,1:T(8,128)}, u32[]{:S(2)}, u32[]{:S(2)}) %collective-permute-start.2) | collective-permute-done | bytes 1048608 | tf_op jit(solution)/shard_map/ppermute | solution.py:22
  710.7 2.4 broadcast_select_fusion
  713.1 2.7 reshape.584
  715.8 2.3 copy.33
  718.0 2.3 convolution_select_fusion
  721.3 2.1 reshape.574
  723.6 3.5 reshape.579
  727.1 73.7 %all-reduce.18.cloned.1.call-done = f32[512,256]{1,0:T(8,128)} async-done(((f32[512,256]{1,0:T(8,128)}), f32[512,256]{1,0:T(8,128)}) %all-reduce.18.cloned.1.call-update) | async-done | bytes 524304 | tf_op jit(solution)/shard_map/psum | solution.py:12
  800.9 7.0 fusion.3
  807.9 2.9 copy.36
  (138 shorter events, 40.5 us)
Async XLA Ops:
  6.5 129.9 %all-reduce.8.cloned.1.call-start = ((), (), s32[]{:S(2)}) async-start(), calls=%async_computation | async-start | bytes 524288 | tf_op jit(solution)/shard_map/psum | solution.py:12
  6.5 30.5 %collective-permute-start = (bf16[512,512]{1,0:T(8,128)(2,1)}, bf16[512,512]{1,0:T(8,128)(2,1)}, u32[]{:S(2)}, u32[]{:S(2)}) collective-permute-start(bf16[512,512]{1,0:T(8,128)(2,1)} %bitcast.175), channel_id=1, source_target_pairs={{0,64},{64,0},{128,192},{192,128},{256,320},{320,256},{384,448},{4... | collective-permute-start | bytes 1572872 | tf_op jit(solution)/shard_map/ppermute | solution.py:22
  19.5 2.5 copy-start.7
  22.6 26.9 %copy-start.2 = (bf16[1,1024,512]{1,2,0:T(8,128)(2,1)}, bf16[1,1024,512]{1,2,0:T(8,128)(2,1)S(1)}, u32[]{:S(2)}) copy-start(bf16[1,1024,512]{1,2,0:T(8,128)(2,1)S(1)} %copy.20) | copy-start | bytes 3145732
  47.3 2.2 copy-start.4
  50.2 1.3 copy-start.1
  52.3 230.3 %all-reduce.10.cloned.1.call-start = ((), (), s32[]{:S(2)}) async-start(), calls=%async_computation.1 | async-start | bytes 2097152 | tf_op jit(solution)/shard_map/psum | solution.py:12
  179.4 0.6 copy-start.17
  205.2 216.8 %all-reduce.12.cloned.1.call-start = ((), (), s32[]{:S(2)}) async-start(), calls=%async_computation.2 | async-start | bytes 1048576 | tf_op jit(solution)/shard_map/psum | solution.py:12
  282.6 51.5 %collective-permute-start.1 = (f32[1024,256]{0,1:T(8,128)}, f32[1024,256]{0,1:T(8,128)}, u32[]{:S(2)}, u32[]{:S(2)}) collective-permute-start(f32[1024,256]{0,1:T(8,128)} %all-reduce.10.cloned.1.call-done), channel_id=1, source_target_pairs={{0,64},{64,0},{128,192},{192,128},{256,320},{320,256},{384,448},{4... | collective-permute-start | bytes 3145736 | tf_op jit(solution)/shard_map/ppermute | solution.py:22
  342.4 163.7 %all-reduce.14.cloned.1.call-start = ((), (), s32[]{:S(2)}) async-start(), calls=%async_computation.3 | async-start | bytes 524288 | tf_op jit(solution)/shard_map/psum | solution.py:12
  342.6 84.7 %copy-start.11 = (pred[512]{0:T(512)(128)(4,1)}, pred[512]{0:T(512)(128)(4,1)S(1)}, u32[]{:S(2)}) copy-start(pred[512]{0:T(512)(128)(4,1)S(1)} %broadcast_in_dim.217) | copy-start | bytes 1540
  342.7 84.6 %copy-start.13 = (pred[512]{0:T(512)(128)(4,1)}, pred[512]{0:T(512)(128)(4,1)S(1)}, u32[]{:S(2)}) copy-start(pred[512]{0:T(512)(128)(4,1)S(1)} %broadcast_in_dim.199) | copy-start | bytes 1540
  427.3 1.3 copy-start.5
  429.3 229.9 %all-reduce.16.cloned.1.call-start = ((), (), s32[]{:S(2)}) async-start(), calls=%async_computation.4 | async-start | bytes 2097152 | tf_op jit(solution)/shard_map/psum | solution.py:12
  508.2 0.7 copy-start.9
  545.1 2.0 copy-start.8
  555.0 0.7 copy-start.10
  576.2 4.0 copy-start.6
  581.8 219.0 %all-reduce.18.cloned.1.call-start = ((), (), s32[]{:S(2)}) async-start(), calls=%async_computation.5 | async-start | bytes 1048576 | tf_op jit(solution)/shard_map/psum | solution.py:12
  659.2 51.5 %collective-permute-start.2 = (f32[1024,256]{0,1:T(8,128)}, f32[1024,256]{0,1:T(8,128)}, u32[]{:S(2)}, u32[]{:S(2)}) collective-permute-start(f32[1024,256]{0,1:T(8,128)} %all-reduce.16.cloned.1.call-done), channel_id=1, source_target_pairs={{0,64},{64,0},{128,192},{192,128},{256,320},{320,256},{384,448},{4... | collective-permute-start | bytes 3145736 | tf_op jit(solution)/shard_map/ppermute | solution.py:22
  721.3 2.1 copy-start.16
  721.3 2.2 copy-start.15
  723.6 77.2 %copy-start = (f32[1024,256]{0,1:T(8,128)S(1)}, f32[1024,256]{0,1:T(8,128)}, u32[]{:S(2)}) copy-start(f32[1024,256]{0,1:T(8,128)} %broadcast_select_fusion) | copy-start | bytes 3145732
  723.6 77.2 %copy-start.3 = (bf16[1,1024,512]{1,2,0:T(8,128)(2,1)S(1)}, bf16[1,1024,512]{1,2,0:T(8,128)(2,1)}, u32[]{:S(2)}) copy-start(bf16[1,1024,512]{1,2,0:T(8,128)(2,1)} %copy-done.2) | copy-start | bytes 3145732
  723.6 77.2 %copy-start.12 = (pred[512]{0:T(512)(128)(4,1)S(1)}, pred[512]{0:T(512)(128)(4,1)}, u32[]{:S(2)}) copy-start(pred[512]{0:T(512)(128)(4,1)} %copy-done.11) | copy-start | bytes 1540
  723.6 77.2 %copy-start.14 = (pred[512]{0:T(512)(128)(4,1)S(1)}, pred[512]{0:T(512)(128)(4,1)}, u32[]{:S(2)}) copy-start(pred[512]{0:T(512)(128)(4,1)} %copy-done.13) | copy-start | bytes 1540
Sparse Core Ops, SparseCore 0:
  52.4 83.9 all-reduce.7
  205.3 77.2 all-reduce.9
  342.6 79.3 all-reduce.11
  429.5 76.6 all-reduce.13
  582.0 77.2 all-reduce.15
  721.4 79.3 all-reduce.17
where the time goes:
time: 824 us; the launch traced here: 818 us
  waiting for transfers between devices  569 us (69%)
  other arithmetic  122 us (15%)
  local copies, waits for them, and re-layouts  55.5 us (7%)
  matrix products  34.8 us (4%)
  starting transfers between devices  19.5 us (2%)
  between operations  16.8 us (2%)
    psum x6, waiting for transfers between devices, broadcast(): return lax.psum(block, axis)  468 us
    ppermute x3, waiting for transfers between devices, partner(): return lax.ppermute(block, axis, route)  101 us
    another operation x14, other arithmetic, factor_column(): pivot_factor = jnp.linalg.cholesky(pivot_tile)  69.3 us
    another operation x5, other arithmetic, factor_column(): lax.linalg.triangular_solve(pivot_factor, column, left_side=False, lower=...  40.9 us
    ppermute x3, starting transfers between devices, partner(): return lax.ppermute(block, axis, route)  18.7 us
  transfers between devices with their start and end apart: 9, of which 9 were waited for; matrix products, arithmetic and copies ran while one was open for 2% of the time, Pallas kernels for 0%

commit v1 on v0

--- a/solution.py
+++ b/solution.py
@@ -7,9 +7,15 @@
 PANELS = 2
 
 
+def add_all(x, axis):
+    parts = lax.all_gather(x, axis, axis=0, tiled=False)
+    summed = parts.sum(axis=0)
+    return summed
+
+
 def broadcast(block, axis, owner):
     block = jnp.where(lax.axis_index(axis) == owner, block, jnp.zeros_like(block))
-    return lax.psum(block, axis)
+    return add_all(block, axis)
 
 
 def partner(block, axis, stride):

time: 824 us -> 772 us (0.937)
  the two profiles are of different devices: /device:TPU:2 before, /device:TPU:1 now
where the time goes in v1:
time: 772 us; the launch traced here: 764 us
  waiting for transfers between devices  488 us (63%)
  other arithmetic  132 us (17%)
  local copies, waits for them, and re-layouts  68.9 us (9%)
  matrix products  24.6 us (3%)
  starting transfers between devices  23.2 us (3%)
  between operations  16.9 us (2%)
  loops' own time  11 us (1%)
    all_gather x6, waiting for transfers between devices, add_all(): parts = lax.all_gather(x, axis, axis=0, tiled=False)  407 us
    ppermute x3, waiting for transfers between devices, partner(): return lax.ppermute(block, axis, route)  80.7 us
    another operation x14, other arithmetic, factor_column(): pivot_factor = jnp.linalg.cholesky(pivot_tile)  69.3 us
    another operation x5, other arithmetic, factor_column(): lax.linalg.triangular_solve(pivot_factor, column, left_side=False, lower=...  41 us
    unnamed x30, local copies, waits for them, and re-layouts  27.4 us
    ppermute x3, starting transfers between devices, partner(): return lax.ppermute(block, axis, route)  22.2 us
  transfers between devices with their start and end apart: 9, of which 9 were waited for; matrix products, arithmetic and copies ran while one was open for 3% of the time, Pallas kernels for 0%

profile of v1, /device:TPU:1, one launch (start us, length us, event | category | flops | bytes accessed | tf_op | source)
XLA Modules:
  0.0 764.4 jit_solution(6530106720673817399)
XLA Ops:
  6.5 8.3 %collective-permute-start = (bf16[512,512]{1,0:T(8,128)(2,1)}, bf16[512,512]{1,0:T(8,128)(2,1)S(1)}, u32[]{:S(2)}, u32[]{:S(2)}) collective-permute-start(bf16[512,512]{1,0:T(8,128)(2,1)} %bitcast.180), channel_id=1, source_target_pairs={{0,64},{64,0},{128,192},{192,128},{256,320},{320,256},{384,448},{4... | collective-permute-start | bytes 1572872 | tf_op jit(solution)/shard_map/ppermute | solution.py:28
  20.6 1.6 copy.42
  23.0 6.5 collective-permute-done
  31.4 1.6 copy.43
  34.9 1.3 copy-done.4
  37.6 53.7 %all-gather.15.cloned.1.call-done = f32[2048,256]{1,0:T(8,128)} async-done(((f32[256,256]{1,0:T(8,128)}), f32[2048,256]{1,0:T(8,128)}) %all-gather.15.cloned.1.call-update) | async-done | bytes 2097168 | tf_op jit(solution)/shard_map/all_gather | solution.py:11
  91.2 1.8 reduce_sum.54
  93.2 11.7 %cholesky.130 = f32[128,128]{1,0:T(8,128)S(1)} custom-call(f32[128,128]{1,0:T(8,128)S(1)} %cholesky.194), custom_call_target="Cholesky" | custom-call | tf_op jit(solution)/shard_map/jit(cholesky)/cholesky | solution.py:80
  105.0 9.8 %custom-call.13 = f32[1,128,128]{1,2,0:T(8,128)S(1)} custom-call(f32[1,128,128]{2,1,0:T(8,128)S(1)} %get-tuple-element.62), custom_call_target="InvertDiagBlocksLowerTriangular" | custom-call | tf_op jit(solution)/shard_map/jit(cholesky)/cholesky | solution.py:80
  115.3 11.7 %cholesky.147 = f32[128,128]{1,0:T(8,128)S(1)} custom-call(f32[128,128]{1,0:T(8,128)S(1)} %convolution_subtract_fusion.3), custom_call_target="Cholesky" | custom-call | tf_op jit(solution)/shard_map/jit(cholesky)/cholesky | solution.py:80
  130.8 15.8 %while.4 = (s32[]{:T(128)}, f32[256,256]{1,0:T(8,128)S(1)}, s32[2,2]{1,0:T(2,128)}, f32[2,128,128]{2,1,0:T(8,128)S(1)}, s32[]{:T(128)}) while((s32[]{:T(128)}, f32[256,256]{1,0:T(8,128)S(1)}, s32[2,2]{1,0:T(2,128)}, f32[2,128,128]{2,1,0:T(8,128)S(1)}, s32[]{:T(128)}) %tuple.56), condition=%wide.while_cond, body=%wide.while_body.sunk | while | flops 2 | bytes 131181 | solution.py:81
  147.3 20.5 %custom-call.14 = f32[2,128,128]{1,2,0:T(8,128)S(1)} custom-call(f32[2,128,128]{2,1,0:T(8,128)} %copy-done.8), custom_call_target="InvertDiagBlocksLowerTriangular" | custom-call | tf_op jit(solution)/shard_map/triangular_solve/custom-call.0 | solution.py:81
  171.3 96.8 %all-gather.17.cloned.1.call-done = f32[8192,256]{0,1:T(8,128)} async-done(((f32[1024,256]{0,1:T(8,128)}), f32[8192,256]{0,1:T(8,128)}) %all-gather.17.cloned.1.call-update) | async-done | bytes 8388624 | tf_op jit(solution)/shard_map/all_gather | solution.py:11
  268.1 10.9 %copy.72 = f32[32,8,8,1024]{3,2,1,0:T(8,128)S(1)} copy(f32[32,8,8,1024]{3,1,2,0:T(8,128)} %bitcast.160) | data formatting | bytes 16777216
  279.0 2.1 bitcast_reduce_fusion.1
  281.1 7.0 collective-permute-start.1
  288.1 37.1 %collective-permute-done.1 = f32[1024,256]{0,1:T(8,128)S(1)} collective-permute-done((f32[1024,256]{0,1:T(8,128)S(1)}, f32[1024,256]{0,1:T(8,128)S(1)}, u32[]{:S(2)}, u32[]{:S(2)}) %collective-permute-start.1) | collective-permute-done | bytes 1048608 | tf_op jit(solution)/shard_map/ppermute | solution.py:28
  325.9 1.4 copy.46
  327.3 2.5 convolution_select_fusion.1
  330.8 1.8 copy.36
  332.6 2.6 copy.62
  335.2 3.1 copy.38
  338.2 1.7 copy.40
  340.0 3.0 copy.41
  342.9 55.4 %all-gather.11.cloned.1.call-done = f32[8,512,256]{2,1,0:T(8,128)} async-done(((f32[1,512,256]{2,1,0:T(8,128)}), f32[8,512,256]{2,1,0:T(8,128)}) %all-gather.11.cloned.1.call-update) | async-done | bytes 4194320 | tf_op jit(solution)/shard_map/all_gather | solution.py:11
  398.3 3.3 reduce_sum.56
  401.6 5.2 select_select_fusion.1
  409.5 37.1 %all-gather.19.cloned.1.call-done = f32[2048,256]{1,0:T(8,128)} async-done(((f32[256,256]{1,0:T(8,128)}), f32[2048,256]{1,0:T(8,128)}) %all-gather.19.cloned.1.call-update) | async-done | bytes 2097168 | tf_op jit(solution)/shard_map/all_gather | solution.py:11
  446.6 1.8 reduce_sum.57
  448.6 11.7 %cholesky.164 = f32[128,128]{1,0:T(8,128)S(1)} custom-call(f32[128,128]{1,0:T(8,128)S(1)} %cholesky.197), custom_call_target="Cholesky" | custom-call | tf_op jit(solution)/shard_map/jit(cholesky)/cholesky | solution.py:80
  460.3 9.8 %custom-call.15 = f32[1,128,128]{1,2,0:T(8,128)S(1)} custom-call(f32[1,128,128]{2,1,0:T(8,128)S(1)} %get-tuple-element.58), custom_call_target="InvertDiagBlocksLowerTriangular" | custom-call | tf_op jit(solution)/shard_map/jit(cholesky)/cholesky | solution.py:80
  470.6 11.7 %cholesky.181 = f32[128,128]{1,0:T(8,128)S(1)} custom-call(f32[128,128]{1,0:T(8,128)S(1)} %convolution_subtract_fusion.2), custom_call_target="Cholesky" | custom-call | tf_op jit(solution)/shard_map/jit(cholesky)/cholesky | solution.py:80
  485.6 5.5 while.5
  491.7 20.5 %custom-call.16 = f32[2,128,128]{1,2,0:T(8,128)S(1)} custom-call(f32[2,128,128]{2,1,0:T(8,128)} %copy-done.9), custom_call_target="InvertDiagBlocksLowerTriangular" | custom-call | tf_op jit(solution)/shard_map/triangular_solve/custom-call.0 | solution.py:81
  512.8 2.0 convolution_subtract_fusion
  516.8 96.8 %all-gather.21.cloned.1.call-done = f32[8192,256]{0,1:T(8,128)} async-done(((f32[1024,256]{0,1:T(8,128)}), f32[8192,256]{0,1:T(8,128)}) %all-gather.21.cloned.1.call-update) | async-done | bytes 8388624 | tf_op jit(solution)/shard_map/all_gather | solution.py:11
  613.5 10.9 %copy.74 = f32[32,8,8,1024]{3,2,1,0:T(8,128)S(1)} copy(f32[32,8,8,1024]{3,1,2,0:T(8,128)} %bitcast.161) | data formatting | bytes 16777216
  624.5 2.1 bitcast_reduce_fusion
  626.6 7.0 collective-permute-start.2
  633.6 37.1 %collective-permute-done.2 = f32[1024,256]{0,1:T(8,128)} collective-permute-done((f32[1024,256]{0,1:T(8,128)S(1)}, f32[1024,256]{0,1:T(8,128)}, u32[]{:S(2)}, u32[]{:S(2)}) %collective-permute-start.2) | collective-permute-done | bytes 1048608 | tf_op jit(solution)/shard_map/ppermute | solution.py:28
  670.7 1.4 broadcast_select_fusion
  672.1 1.4 reshape.586
  673.5 2.3 copy.52
  675.8 2.3 convolution_select_fusion
  679.0 67.7 %all-gather.13.cloned.1.call-done = f32[8,512,256]{2,1,0:T(8,128)} async-done(((f32[1,512,256]{2,1,0:T(8,128)}), f32[8,512,256]{2,1,0:T(8,128)}) %all-gather.13.cloned.1.call-update) | async-done | bytes 4194320 | tf_op jit(solution)/shard_map/all_gather | solution.py:11
  746.7 3.3 reduce_sum.59
  750.0 4.5 select_select_fusion
  754.4 2.9 copy.55
  (131 shorter events, 40.0 us)
Async XLA Ops:
  6.5 84.7 %all-gather.15.cloned.1.call-start = ((), (), s32[]{:S(2)}) async-start(), calls=%async_computation.2 | async-start | bytes 2359296 | tf_op jit(solution)/shard_map/all_gather | solution.py:11
  6.5 22.9 %collective-permute-start = (bf16[512,512]{1,0:T(8,128)(2,1)}, bf16[512,512]{1,0:T(8,128)(2,1)S(1)}, u32[]{:S(2)}, u32[]{:S(2)}) collective-permute-start(bf16[512,512]{1,0:T(8,128)(2,1)} %bitcast.180), channel_id=1, source_target_pairs={{0,64},{64,0},{128,192},{192,128},{256,320},{320,256},{384,448},{4... | collective-permute-start | bytes 1572872 | tf_op jit(solution)/shard_map/ppermute | solution.py:28
  20.6 1.6 copy-start
  31.4 1.6 copy-start.2
  33.0 1.2 copy-start.6
  34.9 1.4 copy-start.4
  37.0 231.1 %all-gather.17.cloned.1.call-start = ((), (), s32[]{:S(2)}) async-start(), calls=%async_computation.3 | async-start | bytes 9437184 | tf_op jit(solution)/shard_map/all_gather | solution.py:11
  129.7 38.0 %copy-start.5 = (f32[1024,512]{1,0:T(8,128)S(1)}, f32[1024,512]{1,0:T(8,128)}, u32[]{:S(2)}) copy-start(f32[1024,512]{1,0:T(8,128)} %copy-done.4) | copy-start | bytes 6291460
  146.6 0.7 copy-start.8
  171.3 227.0 %all-gather.11.cloned.1.call-start = ((), (), s32[]{:S(2)}) async-start(), calls=%async_computation | async-start | bytes 4718592 | tf_op jit(solution)/shard_map/all_gather | solution.py:11
  281.1 44.1 %collective-permute-start.1 = (f32[1024,256]{0,1:T(8,128)S(1)}, f32[1024,256]{0,1:T(8,128)S(1)}, u32[]{:S(2)}, u32[]{:S(2)}) collective-permute-start(f32[1024,256]{0,1:T(8,128)S(1)} %bitcast_reduce_fusion.1), channel_id=1, source_target_pairs={{0,64},{64,0},{128,192},{192,128},{256,320},{320,256},{384,448},{4... | collective-permute-start | bytes 3145736 | tf_op jit(solution)/shard_map/ppermute | solution.py:28
  327.3 3.4 copy-start.1
  330.7 115.9 %all-gather.19.cloned.1.call-start = ((), (), s32[]{:S(2)}) async-start(), calls=%async_computation.4 | async-start | bytes 2359296 | tf_op jit(solution)/shard_map/all_gather | solution.py:11
  335.2 3.1 copy-start.3
  407.8 205.8 %all-gather.21.cloned.1.call-start = ((), (), s32[]{:S(2)}) async-start(), calls=%async_computation.5 | async-start | bytes 9437184 | tf_op jit(solution)/shard_map/all_gather | solution.py:11
  491.1 0.6 copy-start.9
  516.7 229.9 %all-gather.13.cloned.1.call-start = ((), (), s32[]{:S(2)}) async-start(), calls=%async_computation.1 | async-start | bytes 4718592 | tf_op jit(solution)/shard_map/all_gather | solution.py:11
  626.6 7.0 copy-start.7
  626.6 44.1 %collective-permute-start.2 = (f32[1024,256]{0,1:T(8,128)S(1)}, f32[1024,256]{0,1:T(8,128)}, u32[]{:S(2)}, u32[]{:S(2)}) collective-permute-start(f32[1024,256]{0,1:T(8,128)S(1)} %bitcast_reduce_fusion), channel_id=1, source_target_pairs={{0,64},{64,0},{128,192},{192,128},{256,320},{320,256},{384,448},{4... | collective-permute-start | bytes 3145736 | tf_op jit(solution)/shard_map/ppermute | solution.py:28
  679.0 71.0 %copy-start.10 = (pred[2]{0:T(512)(128)(4,1)S(1)}, pred[2]{0:T(512)(128)(4,1)}, u32[]{:S(2)}) copy-start(pred[2]{0:T(512)(128)(4,1)} %get-tuple-element.45) | copy-start | bytes 10
Sparse Core Ops, SparseCore 0:
  37.1 54.1 all-gather.14
  171.4 96.6 all-gather.16
  330.8 67.4 all-gather.10
  407.9 38.6 all-gather.18
  516.9 96.6 all-gather.20
  679.1 67.5 all-gather.12
